TPU v7x, 256 devices: a whole 4x4x8 slice. The times are simulated.
256 devices in a mesh: dom: 64 (over z, y, core), quad: 4 (over x).
Axes of the slice: x: 4, y: 4, z: 8, core: 2. Of those that a mesh axis runs over, the one named last changes fastest.
Arguments:
- element_dofs: float32 [56, 9, 65536], P(None, None, ('dom', 'quad')), may hold values from -6 to 6
- star_matrices: float32 [3, 9, 9, 65536], P(None, None, None, ('dom', 'quad')), may hold values from -3 to 3
- face_normals: float32 [3, 4, 65536], P(None, None, ('dom', 'quad')), may hold values from -3 to 3
- wave_speed: float32 [65536], P(('dom', 'quad')), may hold values from 0.5 to 2
- stiffness: float32 [56, 3, 56], replicated, may hold values from -0.75 to 0.75
- face_projection: float32 [4, 21, 56], replicated, may hold values from -0.75 to 0.75
- face_lift: float32 [4, 56, 21], replicated, may hold values from -0.625 to 0.625
- friction_table: float32 [3, 8], replicated, may hold values from 0.2 to 1
- neighbour_index: int32 [4, 65536], P(None, ('dom', 'quad')), may hold values from 0 to 1535, as said below
- orientation: int32 [4, 65536], P(None, ('dom', 'quad')), may hold values from 0 to 5
- send_list: int32 [2, 65536], P(None, ('dom', 'quad')), may hold values from 0 to 1023
- fault_face: int32 [65536], P(('dom', 'quad')), may hold values from 0 to 1023, as said below
- fault_dest: int32 [65536], P(('dom', 'quad')), may hold values from -1 to 32767, as said below
- fault_region: int32 [16384], replicated, may hold values from 0 to 7
Outputs:
- updated_dofs: float32 [56, 9, 65536], P(None, None, ('dom', 'quad'))
Inputs may be any that keep to these rules, and one draw needn't show every extreme that they name: `neighbour_index`: every halo column 1024 to 1535 is named by exactly one face of the partition; the other faces name its own columns. `fault_face`: the faces of one partition's fault slots are distinct, and none of them names a halo column in neighbour_index. `fault_dest`: owner o sits at dom index 8 (o // 4) and quad index o % 4. Every owner, pair and side appears in exactly one live slot over all partitions. At most 8 live slots of one partition name one owner, and for every owner some partition has exactly 8.
All inputs are finite; a program needn't handle non-finite values.
Results may differ from a plain program's by a relative error of at most 0.0003.
Values sent between devices are 32-bit elements; how exact they have to be, the bound alone decides.
A program may use at most 128 MiB of HBM per device.

v0:
```python
import functools
import math

import jax
import jax.numpy as jnp
from jax import lax
from jax.experimental import pallas as pl
from jax.experimental.pallas import tpu as pltpu
from jax.sharding import PartitionSpec as P

ORDER = 6
NEWTON = 8
BASIS = 56
QUANT = 9
ELEM = 256
COLS = 4 * ELEM
ROWS = 24
COMPS = 224
LANES = 256
CODE, PARTNER = 216, 217
f32, bf16 = jnp.float32, jnp.bfloat16
MESH = pl.DeviceIdType.MESH
VMEM_LIMIT = 56 * 1024 * 1024


def iota(shape, dim):
    return lax.broadcasted_iota(jnp.int32, shape, dim)


def one_hot(mask):
    return jnp.where(mask, 1.0, 0.0).astype(bf16)


def split2(x):
    high = x.astype(bf16).astype(f32)
    return jnp.concatenate([high, x - high], axis=0).astype(bf16)


def split3(x):
    high = x.astype(bf16).astype(f32)
    return jnp.concatenate([high, x - high, high], axis=0).astype(bf16)


def dot(a, b):
    return jnp.dot(a, b, preferred_element_type=f32)


def halves(x):
    n = x.shape[0] // 2
    return x[:n] + x[n:]


def to_col(row):
    n = row.shape[1]
    eye = iota((n, n), 0) == iota((n, n), 1)
    return jnp.sum(jnp.where(eye, row, 0.0), axis=1, keepdims=True)


def to_row(col):
    n = col.shape[0]
    eye = iota((n, n), 0) == iota((n, n), 1)
    return jnp.sum(jnp.where(eye, col, 0.0), axis=0, keepdims=True)


def slot_rows(dest, face):
    n = dest.shape[1]
    live = dest >= 0
    owner = jnp.where(live, dest // 1024, 64).astype(f32)
    code = jnp.where(live, dest % 1024, -1).astype(f32)
    owner_col = to_col(owner)
    earlier = (owner_col == owner) & (iota((n, n), 0) < iota((n, n), 1))
    rank = jnp.sum(jnp.where(earlier, 1.0, 0.0), axis=0, keepdims=True)
    place = jnp.where(live, owner * 8.0 + rank, -1.0)
    put = to_col(place) == iota((n, n), 1).astype(f32)
    face_at = jnp.sum(jnp.where(put, to_col(face.astype(f32) + 1.0), 0.0), axis=0, keepdims=True)
    code_at = jnp.sum(jnp.where(put, to_col(code + 1.0), 0.0), axis=0, keepdims=True)
    return face_at - 1.0, code_at - 1.0


def spatial(load, star_ref, kmat_ref, mixed, store):
    for r in range(QUANT):
        mixed[r] = dot(kmat_ref[...], split3(load(r)))
    for tile in range(ELEM // 128):
        lanes = pl.ds(tile * 128, 128)
        for first in range(0, QUANT, 3):
            total = [None] * 3
            for d in range(3):
                for r in range(QUANT):
                    value = mixed[r, pl.ds(d * BASIS, BASIS), lanes]
                    for i in range(3):
                        term = star_ref[d, first + i, pl.ds(r, 1), lanes] * value
                        total[i] = term if total[i] is None else total[i] + term
            for i in range(3):
                store(first + i, lanes, total[i])


def predict_body(
    x_ref, star_ref, kmat_ref, proj_ref, send_ref, face_ref, dest_ref,
    integral_ref, trace_ref, halo_ref, slots_ref, rows_ref, mixed, deriv,
):
    for r in range(QUANT):
        value = x_ref[r]
        deriv[r] = value
        integral_ref[r] = value

    def degree(k, scale):
        scale = scale / (k + 1).astype(f32)

        def store(q, lanes, value):
            deriv[q, :, lanes] = value
            integral_ref[q, :, lanes] += value * scale

        spatial(lambda r: deriv[r], star_ref, kmat_ref, mixed, store)
        return scale

    lax.fori_loop(1, ORDER, degree, jnp.float32(1.0))

    for r in range(QUANT):
        traced = dot(proj_ref[...], split3(integral_ref[r]))
        for f in range(4):
            trace_ref[pl.ds(r * ROWS, ROWS), pl.ds(f * ELEM, ELEM)] = traced[f * ROWS : (f + 1) * ROWS]
    trace_ref[pl.ds(QUANT * ROWS, COMPS - QUANT * ROWS), :] = jnp.zeros((COMPS - QUANT * ROWS, COLS), f32)
    table = split2(trace_ref[...])
    face_at, code_at = slot_rows(dest_ref[...], face_ref[...])
    column = iota((COLS, 256), 0)
    slots = halves(dot(table, one_hot(column == face_at.astype(jnp.int32))))
    slots_ref[...] = slots
    rows = jnp.concatenate([slots, jnp.zeros((LANES - COMPS, 256), f32)], axis=0)
    whole = code_at.astype(jnp.int32)
    partner = jnp.where(whole >= 0, whole + 1 - 2 * (whole % 2), -5).astype(f32)
    row_of = iota((LANES, 256), 0)
    rows = jnp.where(row_of == CODE, code_at, jnp.where(row_of == PARTNER, partner, rows))
    rows_ref[...] = rows.T
    for side in range(2):
        halo_ref[side] = halves(dot(table, one_hot(column == send_ref[pl.ds(side, 1), :])))


def vmem(n):
    return [pl.BlockSpec(memory_space=pltpu.VMEM)] * n


def predict(x, star, kmat, proj, send, face, dest):
    shape = jax.ShapeDtypeStruct
    return pl.pallas_call(
        predict_body,
        out_shape=(
            shape((QUANT, BASIS, ELEM), f32),
            shape((COMPS, COLS), f32),
            shape((2, COMPS, 256), f32),
            shape((COMPS, 256), f32),
            shape((256, LANES), f32),
        ),
        in_specs=vmem(7),
        out_specs=tuple(vmem(5)),
        scratch_shapes=[
            pltpu.VMEM((QUANT, 3 * BASIS, ELEM), f32),
            pltpu.VMEM((QUANT, BASIS, ELEM), f32),
        ],
        compiler_params=pltpu.CompilerParams(vmem_limit_bytes=VMEM_LIMIT),
    )(x, star, kmat, proj, send, face, dest)


def exchange_body(
    rows_ref, halo_ref, back_ref, outer_halo_ref,
    held, replies, halo_in, back,
    halo_send, halo_recv, out_send, out_recv, ring_send, ring_recv, side_send, side_recv, back_send, back_recv, local_sem,
):
    dom, quad = lax.axis_index("dom"), lax.axis_index("quad")
    doms = lax.axis_size("dom")
    block, member = dom // 8, dom % 8
    y, core = member // 2, member % 2
    base = block * 8
    own = block * 4 + quad
    up, down, far = (y + 1) % 4, (y + 3) % 4, (y + 2) % 4
    upper, lower = lax.rem(dom + 1, doms), lax.rem(dom + doms - 1, doms)

    def slot(yy, cc):
        return yy * 2 + cc

    def peer(o):
        return ((o // 4) * 8 + member, o % 4)

    barrier = pltpu.get_barrier_semaphore()

    def greet(i, carry):
        o = lax.rem(own + i, 32)
        pl.semaphore_signal(barrier, inc=1, device_id=peer(o), device_id_type=MESH)
        return carry

    lax.fori_loop(1, 32, greet, 0)
    neighbours = [(base + slot(up, core), quad), (base + slot(down, core), quad), (base + slot(y, 1 - core), quad), (upper, quad), (lower, quad)]
    for device in neighbours:
        pl.semaphore_signal(barrier, inc=1, device_id=device, device_id_type=MESH)
    pl.semaphore_wait(barrier, 31 + 5)

    def remote(src, dst, send_sem, recv_sem, device):
        return pltpu.make_async_remote_copy(
            src_ref=src, dst_ref=dst, send_sem=send_sem, recv_sem=recv_sem, device_id=device, device_id_type=MESH
        )

    def push(i, carry):
        o = lax.rem(own + i, 32)
        remote(rows_ref.at[o], held.at[member, own], out_send, out_recv, peer(o)).start()
        return carry

    lax.fori_loop(1, 32, push, 0)
    mine = pltpu.make_async_copy(rows_ref.at[own], held.at[member, own], local_sem)
    mine.start()
    low = remote(halo_ref.at[0], halo_in.at[1], halo_send.at[0], halo_recv.at[1], (lower, quad))
    high = remote(halo_ref.at[1], halo_in.at[0], halo_send.at[1], halo_recv.at[0], (upper, quad))
    low.start()
    high.start()
    mine.wait()
    all_but_one = remote(rows_ref.at[pl.ds(0, 31)], held.at[member, pl.ds(0, 31)], out_send, out_recv, peer(own))
    all_but_one.wait_send()
    all_but_one.wait_recv()

    mem_down, mem_up, mem_far = slot(down, core), slot(up, core), slot(far, core)
    to_up, to_down, to_side = neighbours[0], neighbours[1], neighbours[2]
    first, second = pl.ds(0, 16), pl.ds(16, 16)
    ring = [
        remote(held.at[member], held.at[member], ring_send.at[0], ring_recv.at[0], to_up),
        remote(held.at[member], held.at[member], ring_send.at[1], ring_recv.at[1], to_down),
    ]
    side = [remote(held.at[member], held.at[member], side_send.at[0], side_recv.at[0], to_side)]
    ring[0].start()
    ring[1].start()
    side[0].start()

    want = held[member].reshape(256, LANES)[:, PARTNER : PARTNER + 1]

    def matched(m):
        rows = held[m].reshape(256, LANES)
        code = to_row(rows[:, CODE : CODE + 1])
        pick = one_hot(want == code)
        high = rows.astype(bf16)
        low = (rows - high.astype(f32)).astype(bf16)
        return dot(pick, high) + dot(pick, low)

    total = matched(member)
    arrived = remote(held.at[mem_down], held.at[mem_down], ring_send.at[0], ring_recv.at[0], to_up)
    arrived.wait_recv()
    ring.append(remote(held.at[mem_down, first], held.at[mem_down, first], ring_send.at[2], ring_recv.at[2], to_up))
    ring[2].start()
    side.append(remote(held.at[mem_down], held.at[mem_down], side_send.at[1], side_recv.at[1], to_side))
    side[1].start()
    arrived = remote(held.at[mem_up], held.at[mem_up], ring_send.at[1], ring_recv.at[1], to_down)
    arrived.wait_recv()
    ring.append(remote(held.at[mem_up, second], held.at[mem_up, second], ring_send.at[3], ring_recv.at[3], to_down))
    ring[3].start()
    side.append(remote(held.at[mem_up], held.at[mem_up], side_send.at[2], side_recv.at[2], to_side))
    side[2].start()
    total += matched(mem_down)
    total += matched(mem_up)
    side_mem = [slot(yy, 1 - core) for yy in (y, down, up, far)]
    for i in range(3):
        remote(held.at[side_mem[i]], held.at[side_mem[i]], side_send.at[i], side_recv.at[i], to_side).wait_recv()
        total += matched(side_mem[i])
    for i, part in ((2, first), (3, second)):
        remote(held.at[mem_far, part], held.at[mem_far, part], ring_send.at[i], ring_recv.at[i], to_up).wait_recv()
        side.append(remote(held.at[mem_far, part], held.at[mem_far, part], side_send.at[i + 1], side_recv.at[i + 1], to_side))
        side[i + 1].start()
    total += matched(mem_far)
    for i, part in ((3, first), (4, second)):
        remote(held.at[side_mem[3], part], held.at[side_mem[3], part], side_send.at[i], side_recv.at[i], to_side).wait_recv()
    total += matched(side_mem[3])
    replies[...] = total.reshape(32, 8, LANES)

    def reply(i, carry):
        o = lax.rem(own + i, 32)
        remote(replies.at[o], back.at[own], back_send, back_recv, peer(o)).start()
        return carry

    lax.fori_loop(1, 32, reply, 0)
    mine = pltpu.make_async_copy(replies.at[own], back.at[own], local_sem)
    mine.start()
    for copy in ring + side:
        copy.wait_send()
    low.wait_send()
    high.wait_send()
    remote(halo_ref.at[1], halo_in.at[0], halo_send.at[1], halo_recv.at[0], (upper, quad)).wait_recv()
    remote(halo_ref.at[0], halo_in.at[1], halo_send.at[0], halo_recv.at[1], (lower, quad)).wait_recv()
    outer_halo_ref[...] = halo_in[...]
    mine.wait()
    all_but_one = remote(replies.at[pl.ds(0, 31)], back.at[pl.ds(0, 31)], back_send, back_recv, peer(own))
    all_but_one.wait_send()
    all_but_one.wait_recv()
    back_ref[...] = back[...]


def exchange(rows, halo):
    dma = pltpu.SemaphoreType.DMA
    shape = jax.ShapeDtypeStruct
    return pl.pallas_call(
        exchange_body,
        out_shape=(shape((32, 8, LANES), f32), shape((2, COMPS, 256), f32)),
        in_specs=vmem(2),
        out_specs=tuple(vmem(2)),
        scratch_shapes=[
            pltpu.VMEM((8, 32, 8, LANES), f32),
            pltpu.VMEM((32, 8, LANES), f32),
            pltpu.VMEM((2, COMPS, 256), f32),
            pltpu.VMEM((32, 8, LANES), f32),
            dma((2,)), dma((2,)), dma, dma, dma((4,)), dma((4,)), dma((5,)), dma((5,)), dma, dma, dma,
        ],
        compiler_params=pltpu.CompilerParams(collective_id=0, has_side_effects=True, vmem_limit_bytes=VMEM_LIMIT),
    )(rows.reshape(32, 8, LANES), halo)


def inverse_sinh(value):
    magnitude = jnp.abs(value)
    result = jnp.log(magnitude + jnp.sqrt(1.0 + magnitude * magnitude))
    return jnp.where(value < 0.0, -result, result)


def friction_params(code_at, region_ref, table_ref):
    code_col = to_col(code_at).astype(jnp.int32)
    pair = code_col // 2
    n_pairs = region_ref.shape[1]
    regions = jnp.broadcast_to(region_ref[...].astype(f32)[:, None, :], (32, 8, n_pairs)).reshape(256, n_pairs)
    hit = (pair == iota((256, n_pairs), 1)) & (code_col >= 0)
    region = to_row(jnp.sum(jnp.where(hit, regions, 0.0), axis=1, keepdims=True))
    params = []
    for row in range(3):
        value = jnp.full((1, 256), table_ref[row, 0], f32)
        for j in range(1, 8):
            value = jnp.where(region == float(j), table_ref[row, j], value)
        params.append(value)
    return params


def friction(own, other, code_at, params):
    rate_term, state_term, shear = params
    background = 3.0 * shear

    def comp(x, r):
        return x[r * ROWS : (r + 1) * ROWS]

    second = (code_at.astype(jnp.int32) % 2) == 1
    sign = jnp.where(second, -1.0, 1.0)
    pressure = 1.0 + jax.nn.softplus(2.0 - 0.5 * (comp(own, 0) + comp(other, 0)))
    locked = (
        0.5 * (comp(own, 3) + comp(other, 3)) + 0.5 * sign * (comp(other, 7) - comp(own, 7)) + background
    )
    stiff_rate = 0.5 * jnp.exp(state_term / rate_term)
    slip = jnp.zeros_like(locked)
    for _ in range(NEWTON):
        argument = stiff_rate * slip
        mismatch = 0.5 * slip + pressure * rate_term * inverse_sinh(argument) - locked
        gradient = 0.5 + pressure * rate_term * stiff_rate / jnp.sqrt(1.0 + argument * argument)
        slip = slip - 0.4 * mismatch / gradient
    third = 2.0 * (locked - 0.5 * slip - background) - comp(own, 3)
    seventh = comp(other, 7) - sign * slip
    return jnp.concatenate(
        [other[: 3 * ROWS], third, other[4 * ROWS : 7 * ROWS], seventh, other[8 * ROWS : QUANT * ROWS]], axis=0
    )


def flip(x):
    index = 7 - iota((8, 128), 0)
    parts = [
        jnp.take_along_axis(x[:, c : c + 128], index, axis=0, mode="promise_in_bounds") for c in range(0, x.shape[1], 128)
    ]
    return jnp.concatenate(parts, axis=1)


def finish_body(
    x_ref, star_ref, kmat_ref, lift_ref, integral_ref, trace_ref, halo_ref, slots_ref, back_ref,
    index_ref, orient_ref, normals_ref, speed_ref, face_ref, dest_ref, region_ref, table_ref,
    out_ref, mixed, volume, outer, matrix, fluxes,
):
    face_at, code_at = slot_rows(dest_ref[...], face_ref[...])
    other = back_ref[...].reshape(256, LANES).T
    params = friction_params(code_at, region_ref, table_ref)
    imposed = split2(
        jnp.concatenate(
            [friction(slots_ref[...], other, code_at, params), jnp.zeros((COMPS - QUANT * ROWS, 256), f32)], axis=0
        )
    )
    face_col = to_col(face_at).astype(jnp.int32)
    table = split2(trace_ref[...])
    halo = [split2(halo_ref[0]), split2(halo_ref[1])]
    first = iota((8, ELEM), 0) == 0
    for f in range(4):
        cols = pl.ds(f * ELEM, ELEM)
        index = index_ref[pl.ds(f, 1), :]
        raw = dot(table, one_hot(iota((COLS, ELEM), 0) == index))
        for side in range(2):
            raw += dot(halo[side], one_hot(iota((256, ELEM), 0) + (COLS + 256 * side) == index))
        raw = halves(raw)
        put = face_col == iota((256, ELEM), 1) + f * ELEM
        fault = halves(dot(imposed, one_hot(put)))
        is_fault = jnp.sum(jnp.where(put, 1.0, 0.0), axis=0, keepdims=True) > 0.5
        orient = orient_ref[pl.ds(f, 1), :]
        turn = orient % 3
        back = orient >= 3
        for r in range(QUANT):
            group = [raw[r * ROWS + 8 * g : r * ROWS + 8 * g + 8] for g in range(3)]
            moved = [
                jnp.where(turn == 0, group[g], jnp.where(turn == 1, group[(g + 1) % 3], group[(g + 2) % 3]))
                for g in range(3)
            ]
            for g in range(3):
                reverse = jnp.where(first, moved[(3 - g) % 3], flip(moved[(5 - g) % 3]))
                value = jnp.where(back, reverse, moved[g])
                at = r * ROWS + 8 * g
                outer[pl.ds(at, 8), cols] = jnp.where(is_fault, fault[at : at + 8], value)

    for f in range(4):
        for r in range(QUANT):
            total = normals_ref[0, pl.ds(f, 1), :] * star_ref[0, r]
            for d in range(1, 3):
                total += normals_ref[d, pl.ds(f, 1), :] * star_ref[d, r]
            matrix[f, r] = 0.5 * total

    for f in range(4):
        for tile in range(ELEM // 128):
            lanes = pl.ds(tile * 128, 128)
            cols = pl.ds(f * ELEM + tile * 128, 128)
            speed = 0.5 * speed_ref[:, lanes]
            for chunk in range(3):
                at = [pl.ds(r * ROWS + 8 * chunk, 8) for r in range(QUANT)]
                summed = [trace_ref[at[t], cols] + outer[at[t], cols] for t in range(QUANT)]
                for r in range(QUANT):
                    total = speed * (trace_ref[at[r], cols] - outer[at[r], cols])
                    for t in range(QUANT):
                        total += matrix[f, r, pl.ds(t, 1), lanes] * summed[t]
                    fluxes[r, pl.ds(f * ROWS + 8 * chunk, 8), lanes] = total

    def store(q, lanes, value):
        volume[q, :, lanes] = value

    spatial(lambda r: integral_ref[r], star_ref, kmat_ref, mixed, store)
    for r in range(QUANT):
        lifted = dot(lift_ref[...], split3(fluxes[r]))
        out_ref[r] = x_ref[r] + 0.25 * (volume[r] - lifted)


def finish(x, star, kmat, lift, integral, trace, halo, slots, back, index, orient, normals, speed, face, dest, region, table):
    return pl.pallas_call(
        finish_body,
        out_shape=jax.ShapeDtypeStruct((QUANT, BASIS, ELEM), f32),
        in_specs=vmem(16) + [pl.BlockSpec(memory_space=pltpu.SMEM)],
        out_specs=vmem(1)[0],
        scratch_shapes=[
            pltpu.VMEM((QUANT, 3 * BASIS, ELEM), f32),
            pltpu.VMEM((QUANT, BASIS, ELEM), f32),
            pltpu.VMEM((COMPS, COLS), f32),
            pltpu.VMEM((4, QUANT, QUANT, ELEM), f32),
            pltpu.VMEM((QUANT, 4 * ROWS, ELEM), f32),
        ],
        compiler_params=pltpu.CompilerParams(vmem_limit_bytes=VMEM_LIMIT),
    )(x, star, kmat, lift, integral, trace, halo, slots, back, index, orient, normals, speed, face, dest, region, table)


def parts(weights):
    high = lax.reduce_precision(weights, 8, 7)
    return jnp.concatenate([high, high, weights - high], axis=-1).astype(bf16)


def weights_of(stiffness, face_projection, face_lift):
    kmat = parts(jnp.transpose(stiffness, (1, 0, 2)).reshape(3 * BASIS, BASIS))
    pad = ((0, 0), (0, 0), (0, 1), (0, 0))
    proj = parts(jnp.pad(face_projection.reshape(4, 3, 7, BASIS), pad).reshape(4 * ROWS, BASIS))
    lift = jnp.pad(jnp.transpose(face_lift, (1, 0, 2)).reshape(BASIS, 4, 3, 7), ((0, 0), (0, 0), (0, 0), (0, 1)))
    return kmat, proj, parts(lift.reshape(BASIS, 4 * ROWS))


def local(
    element_dofs, star_matrices, face_normals, wave_speed, stiffness, face_projection, face_lift, friction_table,
    neighbour_index, orientation, send_list, fault_face, fault_dest, fault_region,
):
    kmat, proj, lift = weights_of(stiffness, face_projection, face_lift)
    x = jnp.transpose(element_dofs, (1, 0, 2))
    face, dest = fault_face.reshape(1, -1), fault_dest.reshape(1, -1)
    integral, trace, halo, slots, rows = predict(x, star_matrices, kmat, proj, send_list, face, dest)
    back, outer_halo = exchange(rows, halo)
    out = finish(
        x, star_matrices, kmat, lift, integral, trace, outer_halo, slots, back, neighbour_index, orientation,
        face_normals, wave_speed.reshape(1, -1), face, dest, fault_region.reshape(32, -1), friction_table,
    )
    return jnp.transpose(out, (1, 0, 2))


def solution(mesh):
    return jax.shard_map(
        local,
        mesh=mesh,
        in_specs=(
            P(None, None, ("dom", "quad")),
            P(None, None, None, ("dom", "quad")),
            P(None, None, ("dom", "quad")),
            P(("dom", "quad")),
            P(),
            P(),
            P(),
            P(),
            P(None, ("dom", "quad")),
            P(None, ("dom", "quad")),
            P(None, ("dom", "quad")),
            P(("dom", "quad")),
            P(("dom", "quad")),
            P(),
        ),
        out_specs=P(None, None, ("dom", "quad")),
        check_vma=False,
    )
```

profile of v0, /device:TPU:1, one launch (start us, length us, event | category | flops | bytes accessed | tf_op | source)
XLA Modules:
  0.0 69.6 jit_solution(1937099696699904993)
XLA Ops:
  0.0 0.0 copy-start
  0.0 1.0 %reduce-precision_convert_fusion = (bf16[168,56]{1,0:T(8,128)(2,1)S(1)}, bf16[168,56]{1,0:T(8,128)(2,1)S(1)}) fusion(f32[56,3,56]{2,0,1:T(8,128)} %param.18), kind=kLoop, calls=%fused_computation.1 | loop fusion | flops 37632 | bytes 75264 | tf_op jit(solution)/shard_map/convert.6
  1.0 0.8 %pad_maximum_fusion.kmat_ref = bf16[168,168]{1,0:T(8,128)(2,1)} fusion(bf16[168,56]{1,0:T(8,128)(2,1)S(1)} %get-tuple-element.20, bf16[168,56]{1,0:T(8,128)(2,1)S(1)} %get-tuple-element.19), kind=kLoop, calls=%fused_computation.3 | loop fusion | flops 169344 | bytes 94080 | tf_op jit(solution)/shard_map/concatenate | solution.py:458
  1.7 0.8 %copy.22 = f32[4,3,7,56]{3,2,1,0:T(8,128)S(1)} copy(f32[4,3,7,56]{3,0,2,1:T(4,128)} %bitcast.23) | data formatting | bytes 37632 | tf_op jit(solution)/shard_map/reshape | solution.py:464
  2.5 0.7 %pad_maximum_fusion.1.proj_ref = bf16[96,168]{1,0:T(8,128)(2,1)} fusion(bf16[96,56]{1,0:T(8,128)(2,1)S(1)} %get-tuple-element.22, bf16[96,56]{1,0:T(8,128)(2,1)S(1)} %get-tuple-element.21), kind=kLoop, calls=%fused_computation.7 | loop fusion | flops 96768 | bytes 53760 | tf_op jit(solution)/shard_map/concatenate | solution.py:458
  3.2 0.0 copy-done
  3.2 0.9 %copy.24.star_ref = f32[3,9,9,256]{3,2,1,0:T(8,128)} copy(f32[3,9,9,256]{3,0,2,1:T(4,128)S(1)} %copy-done) | data formatting | bytes 497664 | tf_op args[1]
  4.1 10.9 %shard_map.136 = (f32[9,56,256]{2,1,0:T(8,128)}, f32[224,1024]{1,0:T(8,128)}, f32[2,224,256]{2,1,0:T(8,128)}, f32[224,256]{1,0:T(8,128)}, f32[256,256]{1,0:T(8,128)}) custom-call(f32[9,56,256]{2,1,0:T(8,128)} %bitcast.19, f32[3,9,9,256]{3,2,1,0:T(8,128)} %copy.24.star_ref, bf16[168,168]{1,0:T(8,128)(2,1)} %pad_maximum_fusion.kmat_ref, ...), custom_call_target="tpu_custom_call" | custom-call | tf_op jit(solution)/shard_map/pallas_call | solution.py:144
  15.0 0.0 copy-start.2
  15.0 45.4 %shard_map.137 = (f32[32,8,256]{2,1,0:T(8,128)}, f32[2,224,256]{2,1,0:T(8,128)}) custom-call(f32[32,8,256]{2,1,0:T(8,128)} %bitcast.21, f32[2,224,256]{2,1,0:T(8,128)} %get-tuple-element.15.halo_ref), custom_call_target="tpu_custom_call" | custom-call | tf_op jit(solution)/shard_map/pallas_call | solution.py:294
  60.4 0.0 copy-done.2
  60.5 0.1 copy.20
  60.6 0.0 copy-start.1
  60.6 0.7 %pad_maximum_fusion.2.lift_ref = bf16[56,288]{1,0:T(8,128)(2,1)} fusion(bf16[56,96]{1,0:T(8,128)(2,1)S(1)} %get-tuple-element.24, bf16[56,96]{1,0:T(8,128)(2,1)S(1)} %get-tuple-element.23), kind=kLoop, calls=%fused_computation.8 | loop fusion | flops 96768 | bytes 53760 | tf_op jit(solution)/shard_map/concatenate | solution.py:458
  61.3 0.1 copy-done.1
  61.4 0.6 reshape.39.region_ref
  62.0 7.6 %shard_map.138 = f32[9,56,256]{2,1,0:T(8,128)} custom-call(f32[9,56,256]{2,1,0:T(8,128)} %bitcast.20, f32[3,9,9,256]{3,2,1,0:T(8,128)} %copy.24.star_ref, bf16[168,168]{1,0:T(8,128)(2,1)} %pad_maximum_fusion.kmat_ref, bf16[56,288]{1,0:T(8,128)(2,1)} %pad_maximum_fusion.2.lift_ref, f32[9,56,256]{2,1,0:T(8,128)} %get-tuple-element.12.integral_ref, ...), custom_call_target="tpu_custom_call" | custom-call | tf_op jit(solution)/shard_map/pallas_call | solution.py:440
  (5 shorter events, 0.1 us)
Async XLA Ops:
  0.0 3.2 %copy-start = (f32[3,9,9,256]{3,0,2,1:T(4,128)S(1)}, f32[3,9,9,256]{3,0,2,1:T(4,128)}, u32[]{:S(2)}) copy-start(f32[3,9,9,256]{3,0,2,1:T(4,128)} %param.15) | copy-start | bytes 746500
  15.0 45.4 %copy-start.2 = (f32[4,56,21]{1,0,2:T(4,128)S(1)}, f32[4,56,21]{1,0,2:T(4,128)}, u32[]{:S(2)}) copy-start(f32[4,56,21]{1,0,2:T(4,128)} %param.20) | copy-start | bytes 56452
  60.6 0.9 %copy-start.1 = (s32[16384]{0:T(1024)S(1)}, s32[16384]{0:T(1024)}, u32[]{:S(2)}) copy-start(s32[16384]{0:T(1024)} %param.27) | copy-start | bytes 196612
where the time goes:
time: 70 us; the launch traced here: 69.6 us
  Pallas kernels  63.9 us (91%)
  other arithmetic  3.15 us (4%)
  local copies, waits for them, and re-layouts  2.5 us (4%)
    pallas_call x1, Pallas kernels, exchange(): pl.pallas_call(exchange_body, out_shape=(shape((32, 8, LANES), f32), shap...  45.4 us
    pallas_call x1, Pallas kernels, predict(): pl.pallas_call(predict_body, out_shape=(shape((QUANT, BASIS, ELEM), f32),...  10.9 us
    pallas_call x1, Pallas kernels, finish(): pl.pallas_call(finish_body, out_shape=jax.ShapeDtypeStruct((QUANT, BASIS,...  7.58 us
    concatenate x3, other arithmetic, parts(): return jnp.concatenate([high, high, weights - high], axis=-1).astype(bf16)  2.17 us

commit v1 on v0

v1 whole, which is shorter than its diff:
```python
import functools
import math

import jax
import jax.numpy as jnp
from jax import lax
from jax.experimental import pallas as pl
from jax.experimental.pallas import tpu as pltpu
from jax.sharding import PartitionSpec as P

ORDER = 6
NEWTON = 8
BASIS = 56
QUANT = 9
ELEM = 256
COLS = 4 * ELEM
ROWS = 24
COMPS = 224
WIRE = 192
CODE, PARTNER = 189, 190
PIECES = 4
f32, bf16 = jnp.float32, jnp.bfloat16
MESH = pl.DeviceIdType.MESH
VMEM_LIMIT = 56 * 1024 * 1024


def iota(shape, dim):
    return lax.broadcasted_iota(jnp.int32, shape, dim)


def one_hot(mask):
    return jnp.where(mask, 1.0, 0.0).astype(bf16)


def split2(x):
    high = x.astype(bf16).astype(f32)
    return jnp.concatenate([high, x - high], axis=0).astype(bf16)


def split3(x):
    high = x.astype(bf16).astype(f32)
    return jnp.concatenate([high, x - high, high], axis=0).astype(bf16)


def dot(a, b):
    return jnp.dot(a, b, preferred_element_type=f32)


def halves(x):
    n = x.shape[0] // 2
    return x[:n] + x[n:]


def to_col(row):
    n = row.shape[1]
    eye = iota((n, n), 0) == iota((n, n), 1)
    return jnp.sum(jnp.where(eye, row, 0.0), axis=1, keepdims=True)


def to_row(col):
    n = col.shape[0]
    eye = iota((n, n), 0) == iota((n, n), 1)
    return jnp.sum(jnp.where(eye, col, 0.0), axis=0, keepdims=True)


def slot_rows(dest, face):
    n = dest.shape[1]
    live = dest >= 0
    owner = jnp.where(live, dest // 1024, 64).astype(f32)
    code = jnp.where(live, dest % 1024, -1).astype(f32)
    owner_col = to_col(owner)
    earlier = (owner_col == owner) & (iota((n, n), 0) < iota((n, n), 1))
    rank = jnp.sum(jnp.where(earlier, 1.0, 0.0), axis=0, keepdims=True)
    place = jnp.where(live, owner * 8.0 + rank, -1.0)
    put = to_col(place) == iota((n, n), 1).astype(f32)
    face_at = jnp.sum(jnp.where(put, to_col(face.astype(f32) + 1.0), 0.0), axis=0, keepdims=True)
    code_at = jnp.sum(jnp.where(put, to_col(code + 1.0), 0.0), axis=0, keepdims=True)
    return face_at - 1.0, code_at - 1.0


def packed(first, second):
    swapped = pltpu.roll(pltpu.roll(second, 64, 1), 252, 0)
    pairs = jnp.where(iota((256, 128), 1) < 64, second, swapped)
    return first.reshape(32, 8, 128), pairs.reshape(32, 8, 128)[:, :4, :]


def put_packed(ref, first, second):
    ref[:, pl.ds(0, 8), :], ref[:, pl.ds(8, 4), :] = packed(first, second)


def unpacked(ref, *at):
    first = ref[(*at, slice(None), pl.ds(0, 8), slice(None))].reshape(256, 128)
    pairs = ref[(*at, slice(None), pl.ds(8, 4), slice(None))]
    pairs = jnp.concatenate([pairs, pairs], axis=1).reshape(256, 128)
    second = jnp.where(iota((256, 128), 0) % 8 < 4, pairs, pltpu.roll(pairs, 64, 1))
    return first, second


def narrow():
    value, row = iota((WIRE, 2 * COMPS), 0), iota((WIRE, 2 * COMPS), 1)
    row = jnp.where(row >= COMPS, row - COMPS, row)
    return one_hot((row == value + ((value * 9363) >> 16)) & (value < CODE))


def widen():
    row, value = iota((COMPS, 2 * WIRE), 0), iota((COMPS, 2 * WIRE), 1)
    value = jnp.where(value >= WIRE, value - WIRE, value)
    return one_hot((row == value + ((value * 9363) >> 16)) & (value < CODE))


def weight_parts(weights):
    high = weights.astype(bf16).astype(f32)
    return jnp.concatenate([high, high, weights - high], axis=1).astype(bf16)


def spatial_products(load, kmat_ref, mixed):
    for r in range(QUANT):
        mixed[r] = dot(kmat_ref[...], split3(load(r)))


def spatial_mix(tile, firsts, star_ref, mixed, store):
    lanes = pl.ds(tile * 128, 128)
    for first in firsts:
        total = [None] * 3
        for d in range(3):
            for r in range(QUANT):
                value = mixed[r, pl.ds(d * BASIS, BASIS), lanes]
                for i in range(3):
                    term = star_ref[d, first + i, pl.ds(r, 1), lanes] * value
                    total[i] = term if total[i] is None else total[i] + term
        for i in range(3):
            store(first + i, lanes, total[i])


def inverse_sinh(value):
    magnitude = jnp.abs(value)
    result = jnp.log(magnitude + jnp.sqrt(1.0 + magnitude * magnitude))
    return jnp.where(value < 0.0, -result, result)


def friction_params(code_at, region_ref, table_ref):
    code_col = to_col(code_at).astype(jnp.int32)
    pairs = region_ref.shape[1] // 32
    regions = jnp.concatenate(
        [jnp.broadcast_to(region_ref[:, pl.ds(o * pairs, pairs)], (8, pairs)) for o in range(32)], axis=0
    ).astype(f32)
    hit = (code_col // 2 == iota((256, pairs), 1)) & (code_col >= 0)
    region = to_row(jnp.sum(jnp.where(hit, regions, 0.0), axis=1, keepdims=True))
    params = []
    for row in range(3):
        value = jnp.full((1, 256), table_ref[row, 0], f32)
        for j in range(1, 8):
            value = jnp.where(region == float(j), table_ref[row, j], value)
        params.append(value)
    return params


def friction(own, other, code_at, params):
    rate_term, state_term, shear = params
    background = 3.0 * shear

    def comp(x, r):
        return x[r * ROWS : (r + 1) * ROWS]

    second = (code_at.astype(jnp.int32) % 2) == 1
    sign = jnp.where(second, -1.0, 1.0)
    pressure = 1.0 + jax.nn.softplus(2.0 - 0.5 * (comp(own, 0) + comp(other, 0)))
    locked = (
        0.5 * (comp(own, 3) + comp(other, 3)) + 0.5 * sign * (comp(other, 7) - comp(own, 7)) + background
    )
    stiff_rate = 0.5 * jnp.exp(state_term / rate_term)
    slip = jnp.zeros_like(locked)
    for _ in range(NEWTON):
        argument = stiff_rate * slip
        mismatch = 0.5 * slip + pressure * rate_term * inverse_sinh(argument) - locked
        gradient = 0.5 + pressure * rate_term * stiff_rate / jnp.sqrt(1.0 + argument * argument)
        slip = slip - 0.4 * mismatch / gradient
    third = 2.0 * (locked - 0.5 * slip - background) - comp(own, 3)
    seventh = comp(other, 7) - sign * slip
    return jnp.concatenate(
        [other[: 3 * ROWS], third, other[4 * ROWS : 7 * ROWS], seventh, other[8 * ROWS : QUANT * ROWS]], axis=0
    )


def flip(x):
    index = 7 - iota((8, 128), 0)
    parts = [
        jnp.take_along_axis(x[:, c : c + 128], index, axis=0, mode="promise_in_bounds") for c in range(0, x.shape[1], 128)
    ]
    return jnp.concatenate(parts, axis=1)


def step_body(
    x_ref, star_in, stiff_ref, proj_in, lift_in, normals_ref, speed_ref, index_ref, orient_ref, send_ref, face_ref,
    dest_ref, region_ref, table_ref,
    change_ref,
    star, kmat, proj, lift, mixed, deriv, integral, volume, trace, table, slots, raw, matrix, fluxes, points, params,
    rows, held, replies, back, halo_out, halo_in,
    halo_send, halo_recv, out_send, out_recv, ring_send, ring_recv, side_send, side_recv, back_send, back_recv, local_sem,
):
    dom, quad = lax.axis_index("dom"), lax.axis_index("quad")
    doms = lax.axis_size("dom")
    block, member = dom // 8, dom % 8
    y, core = member // 2, member % 2
    own = block * 4 + quad

    def slot(yy, cc):
        return yy * 2 + cc

    def peer(o):
        return ((o // 4) * 8 + member, o % 4)

    up, down, far = (y + 1) % 4, (y + 3) % 4, (y + 2) % 4
    mem_up, mem_down, mem_far = slot(up, core), slot(down, core), slot(far, core)
    to_up, to_down = (block * 8 + mem_up, quad), (block * 8 + mem_down, quad)
    to_side = (block * 8 + slot(y, 1 - core), quad)
    upper, lower = (lax.rem(dom + 1, doms), quad), (lax.rem(dom + doms - 1, doms), quad)

    barrier = pltpu.get_barrier_semaphore()

    def greet(i, carry):
        pl.semaphore_signal(barrier, inc=1, device_id=peer(lax.rem(own + i, 32)), device_id_type=MESH)
        return carry

    lax.fori_loop(1, 32, greet, 0)
    for device in (to_up, to_down, to_side, upper, lower):
        pl.semaphore_signal(barrier, inc=1, device_id=device, device_id_type=MESH)

    for q in range(QUANT):
        for r in range(QUANT):
            star[:, q, r, :] = star_in[q, r]
    kmat[...] = weight_parts(stiff_ref[...])
    for source, padded in ((proj_in, points.at[0]), (lift_in, points.at[1])):
        padded[...] = jnp.zeros_like(padded)
        for p in range(21):
            padded[:, p // 7 * 8 + p % 7, :] = source[p]
    proj[...] = weight_parts(points[0].reshape(4 * ROWS, BASIS))
    lift[...] = weight_parts(
        jnp.concatenate(
            [
                jnp.concatenate([points[1].reshape(4 * ROWS, BASIS), jnp.zeros((4 * ROWS, 128 - BASIS), f32)], axis=1),
                jnp.zeros((128 - 4 * ROWS, 128), f32),
            ],
            axis=0,
        ).T[:BASIS, : 4 * ROWS]
    )
    face_at, code_at = slot_rows(dest_ref[...], face_ref[...])

    for r in range(QUANT):
        value = x_ref[r]
        deriv[r] = value
        integral[r] = value

    def degree(k, scale):
        scale = scale / (k + 1).astype(f32)

        def store(q, lanes, value):
            deriv[q, :, lanes] = value
            integral[q, :, lanes] += value * scale

        spatial_products(lambda r: deriv[r], kmat, mixed)
        for tile in range(2):
            spatial_mix(tile, (0, 3, 6), star, mixed, store)
        return scale

    lax.fori_loop(1, ORDER, degree, jnp.float32(1.0))

    for r in range(QUANT):
        traced = dot(proj[...], split3(integral[r]))
        for f in range(4):
            trace[pl.ds(r * ROWS, ROWS), pl.ds(f * ELEM, ELEM)] = traced[f * ROWS : (f + 1) * ROWS]
    trace[pl.ds(QUANT * ROWS, COMPS - QUANT * ROWS), :] = jnp.zeros((COMPS - QUANT * ROWS, COLS), f32)
    table[...] = split2(trace[...])
    column = iota((COLS, 256), 0)
    slots[...] = halves(dot(table[...], one_hot(column == face_at.astype(jnp.int32))))
    wire = dot(narrow(), split2(slots[...]))
    whole = code_at.astype(jnp.int32)
    partner = jnp.where(whole >= 0, whole + 1 - 2 * (whole % 2), -5).astype(f32)
    at = iota((WIRE, 256), 0)
    wire = jnp.where(at == CODE, code_at, jnp.where(at == PARTNER, partner, wire))
    put_packed(rows, wire[:128].T, jnp.concatenate([wire[128:], wire[128:]], axis=0).T)

    def remote(src, dst, send_sem, recv_sem, device):
        return pltpu.make_async_remote_copy(
            src_ref=src, dst_ref=dst, send_sem=send_sem, recv_sem=recv_sem, device_id=device, device_id_type=MESH
        )

    pl.semaphore_wait(barrier, 31 + 5)
    per = 32 // PIECES

    for piece in range(PIECES):
        def push(i, carry, piece=piece):
            o = lax.rem(own + i, 32)
            remote(rows.at[o], held.at[member, i], out_send, out_recv.at[piece], peer(o)).start()
            return carry

        lax.fori_loop(max(1, piece * per), (piece + 1) * per, push, 0)
    mine = pltpu.make_async_copy(rows.at[own], held.at[member, 0], local_sem)
    mine.start()

    sent = []

    def go(copy):
        copy.start()
        sent.append(copy)

    def part(m, piece):
        return held.at[m, pl.ds(piece * per, per)]

    def ring(m, piece, index, device):
        return remote(part(m, piece), part(m, piece), ring_send.at[index], ring_recv.at[index], device)

    def side(m, piece, index):
        return remote(part(m, piece), part(m, piece), side_send.at[index], side_recv.at[index], to_side)

    def own_piece(piece):
        count = per - 1 if piece == 0 else per
        got = held.at[member, pl.ds(piece * per, count)]
        remote(rows.at[pl.ds(0, count)], got, out_send, out_recv.at[piece], to_up).wait_recv()
        if piece == 0:
            mine.wait()
        go(ring(member, piece, piece, to_up))
        go(ring(member, piece, PIECES + piece, to_down))
        go(side(member, piece, piece))

    def ring_piece(piece):
        ring(mem_down, piece, piece, to_up).wait_recv()
        if piece % 2 == 0:
            go(ring(mem_down, piece, 2 * PIECES + piece, to_up))
        go(side(mem_down, piece, PIECES + piece))
        ring(mem_up, piece, PIECES + piece, to_down).wait_recv()
        if piece % 2 == 1:
            go(ring(mem_up, piece, 2 * PIECES + piece, to_down))
        go(side(mem_up, piece, 2 * PIECES + piece))

    def far_piece(piece):
        ring(mem_far, piece, 2 * PIECES + piece, to_up).wait_recv()
        go(side(mem_far, piece, 3 * PIECES + piece))

    def side_pieces(m, index):
        for piece in range(PIECES):
            side(m, piece, index * PIECES + piece).wait_recv()

    def halo_side(s):
        halo_out[s] = halves(dot(table[...], one_hot(column == send_ref[pl.ds(s, 1), :])))

    def own_neighbours(f):
        index = index_ref[pl.ds(f, 1), :]
        raw[:, pl.ds(f * ELEM, ELEM)] = halves(dot(table[...], one_hot(column == index)))

    def face_matrices(f):
        for r in range(QUANT):
            total = normals_ref[0, pl.ds(f, 1), :] * star[0, r]
            for d in range(1, 3):
                total += normals_ref[d, pl.ds(f, 1), :] * star[d, r]
            matrix[f, r] = 0.5 * total

    def keep_volume(q, lanes, value):
        volume[q, :, lanes] = value

    halo_side(0)
    low = remote(halo_out.at[0], halo_in.at[1], halo_send.at[0], halo_recv.at[1], lower)
    low.start()
    halo_side(1)
    high = remote(halo_out.at[1], halo_in.at[0], halo_send.at[1], halo_recv.at[0], upper)
    high.start()
    for i, row in enumerate(friction_params(code_at, region_ref, table_ref)):
        params[pl.ds(i, 1), :] = row
    own_piece(0)
    own_neighbours(0)
    own_piece(1)
    own_neighbours(1)
    own_piece(2)
    ring_piece(0)
    own_neighbours(2)
    own_piece(3)
    ring_piece(1)

    want = unpacked(held, member)[1][:, PARTNER - 128 : PARTNER - 127]

    def matched(m):
        first, second = unpacked(held, m)
        pick = one_hot(want == to_row(second[:, CODE - 128 : CODE - 127]))
        values = jnp.concatenate([first, second], axis=1)
        high_part = values.astype(bf16)
        low_part = (values - high_part.astype(f32)).astype(bf16)
        return dot(pick, high_part) + dot(pick, low_part)

    total = matched(member)
    ring_piece(2)
    own_neighbours(3)
    ring_piece(3)
    far_piece(0)
    total += matched(mem_down)
    far_piece(1)
    total += matched(mem_up)
    far_piece(2)
    side_pieces(slot(y, 1 - core), 0)
    total += matched(slot(y, 1 - core))
    far_piece(3)
    side_pieces(slot(down, 1 - core), 1)
    total += matched(slot(down, 1 - core))
    side_pieces(slot(up, 1 - core), 2)
    total += matched(slot(up, 1 - core))
    total += matched(mem_far)
    side_pieces(slot(far, 1 - core), 3)
    total += matched(slot(far, 1 - core))
    put_packed(replies, total[:, :128], total[:, 128:])

    def reply(i, carry):
        o = lax.rem(own + 32 - i, 32)
        remote(replies.at[i], back.at[own], back_send, back_recv, peer(o)).start()
        return carry

    lax.fori_loop(1, 32, reply, 0)
    mine = pltpu.make_async_copy(replies.at[0], back.at[own], local_sem)
    mine.start()

    for f in range(4):
        face_matrices(f)
    spatial_products(lambda r: integral[r], kmat, mixed)
    for tile in range(2):
        spatial_mix(tile, (0, 3, 6), star, mixed, keep_volume)

    remote(halo_out.at[1], halo_in.at[0], halo_send.at[1], halo_recv.at[0], upper).wait_recv()
    remote(halo_out.at[0], halo_in.at[1], halo_send.at[0], halo_recv.at[1], lower).wait_recv()
    halo = [split2(halo_in[0]), split2(halo_in[1])]
    first_row = iota((8, ELEM), 0) == 0
    for f in range(4):
        cols = pl.ds(f * ELEM, ELEM)
        index = index_ref[pl.ds(f, 1), :]
        near = dot(halo[0], one_hot(iota((256, ELEM), 0) + COLS == index))
        near += dot(halo[1], one_hot(iota((256, ELEM), 0) + (COLS + 256) == index))
        near = halves(near)
        orient = orient_ref[pl.ds(f, 1), :]
        turn = orient % 3
        reversed_face = orient >= 3
        for r in range(QUANT):
            at = [r * ROWS + 8 * g for g in range(3)]
            group = [raw[pl.ds(a, 8), cols] + near[a : a + 8] for a in at]
            moved = [
                jnp.where(turn == 0, group[g], jnp.where(turn == 1, group[(g + 1) % 3], group[(g + 2) % 3]))
                for g in range(3)
            ]
            for g in range(3):
                reverse = jnp.where(first_row, moved[(3 - g) % 3], flip(moved[(5 - g) % 3]))
                raw[pl.ds(at[g], 8), cols] = jnp.where(reversed_face, reverse, moved[g])
    outer = raw

    for copy in sent:
        copy.wait_send()
    low.wait_send()
    high.wait_send()
    out_done = remote(rows.at[pl.ds(0, 31)], held.at[member, pl.ds(0, 31)], out_send, out_recv.at[0], to_up)
    out_done.wait_send()
    face_col = to_col(face_at).astype(jnp.int32)
    mine.wait()
    returned = remote(replies.at[pl.ds(0, 31)], back.at[pl.ds(0, 31)], back_send, back_recv, to_up)
    returned.wait_send()
    returned.wait_recv()
    first, second = unpacked(back)
    other = dot(widen(), split2(jnp.concatenate([first.T, second.T[: WIRE - 128]], axis=0)))
    law = [params[pl.ds(i, 1), :] for i in range(3)]
    imposed = split2(
        jnp.concatenate(
            [friction(slots[...], other, code_at, law), jnp.zeros((COMPS - QUANT * ROWS, 256), f32)], axis=0
        )
    )

    for f in range(4):
        cols = pl.ds(f * ELEM, ELEM)
        put = face_col == iota((256, ELEM), 1) + f * ELEM
        fault = halves(dot(imposed, one_hot(put)))
        is_fault = jnp.sum(jnp.where(put, 1.0, 0.0), axis=0, keepdims=True) > 0.5
        outer[:, cols] = jnp.where(is_fault, fault, outer[:, cols])
        for tile in range(ELEM // 128):
            lanes = pl.ds(tile * 128, 128)
            cols = pl.ds(f * ELEM + tile * 128, 128)
            speed = 0.5 * speed_ref[:, lanes]
            for chunk in range(3):
                at = [pl.ds(r * ROWS + 8 * chunk, 8) for r in range(QUANT)]
                summed = [trace[at[t], cols] + outer[at[t], cols] for t in range(QUANT)]
                for r in range(QUANT):
                    flux = speed * (trace[at[r], cols] - outer[at[r], cols])
                    for t in range(QUANT):
                        flux += matrix[f, r, pl.ds(t, 1), lanes] * summed[t]
                    fluxes[r, pl.ds(f * ROWS + 8 * chunk, 8), lanes] = flux

    for r in range(QUANT):
        change_ref[r] = 0.25 * (volume[r] - dot(lift[...], split3(fluxes[r])))


def step(*operands):
    vmem, dma = pl.BlockSpec(memory_space=pltpu.VMEM), pltpu.SemaphoreType.DMA
    return pl.pallas_call(
        step_body,
        out_shape=jax.ShapeDtypeStruct((QUANT, BASIS, ELEM), f32),
        in_specs=[vmem] * 13 + [pl.BlockSpec(memory_space=pltpu.SMEM)],
        out_specs=vmem,
        scratch_shapes=[
            pltpu.VMEM((3, QUANT, QUANT, ELEM), f32),
            pltpu.VMEM((3 * BASIS, 3 * BASIS), bf16),
            pltpu.VMEM((4 * ROWS, 3 * BASIS), bf16),
            pltpu.VMEM((BASIS, 12 * ROWS), bf16),
            pltpu.VMEM((QUANT, 3 * BASIS, ELEM), f32),
            pltpu.VMEM((QUANT, BASIS, ELEM), f32),
            pltpu.VMEM((QUANT, BASIS, ELEM), f32),
            pltpu.VMEM((QUANT, BASIS, ELEM), f32),
            pltpu.VMEM((COMPS, COLS), f32),
            pltpu.VMEM((2 * COMPS, COLS), bf16),
            pltpu.VMEM((COMPS, 256), f32),
            pltpu.VMEM((COMPS, COLS), f32),
            pltpu.VMEM((4, QUANT, QUANT, ELEM), f32),
            pltpu.VMEM((QUANT, 4 * ROWS, ELEM), f32),
            pltpu.VMEM((2, 4, ROWS, BASIS), f32),
            pltpu.VMEM((8, 256), f32),
            pltpu.VMEM((32, 12, 128), f32),
            pltpu.VMEM((8, 32, 12, 128), f32),
            pltpu.VMEM((32, 12, 128), f32),
            pltpu.VMEM((32, 12, 128), f32),
            pltpu.VMEM((2, COMPS, 256), f32),
            pltpu.VMEM((2, COMPS, 256), f32),
            dma((2,)), dma((2,)), dma, dma((PIECES,)), dma((3 * PIECES,)), dma((3 * PIECES,)),
            dma((4 * PIECES,)), dma((4 * PIECES,)), dma, dma, dma,
        ],
        compiler_params=pltpu.CompilerParams(collective_id=0, has_side_effects=True, vmem_limit_bytes=VMEM_LIMIT),
    )(*operands)


def local(
    element_dofs, star_matrices, face_normals, wave_speed, stiffness, face_projection, face_lift, friction_table,
    neighbour_index, orientation, send_list, fault_face, fault_dest, fault_region,
):
    change = step(
        jnp.transpose(element_dofs, (1, 0, 2)),
        jnp.transpose(star_matrices, (1, 2, 0, 3)),
        jnp.transpose(stiffness, (1, 0, 2)).reshape(3 * BASIS, BASIS),
        jnp.transpose(face_projection, (1, 0, 2)),
        jnp.transpose(face_lift, (2, 0, 1)),
        face_normals, wave_speed.reshape(1, -1), neighbour_index, orientation, send_list,
        fault_face.reshape(1, -1), fault_dest.reshape(1, -1), fault_region.reshape(1, -1), friction_table,
    )
    return element_dofs + jnp.transpose(change, (1, 0, 2))


def solution(mesh):
    return jax.shard_map(
        local,
        mesh=mesh,
        in_specs=(
            P(None, None, ("dom", "quad")),
            P(None, None, None, ("dom", "quad")),
            P(None, None, ("dom", "quad")),
            P(("dom", "quad")),
            P(),
            P(),
            P(),
            P(),
            P(None, ("dom", "quad")),
            P(None, ("dom", "quad")),
            P(None, ("dom", "quad")),
            P(("dom", "quad")),
            P(("dom", "quad")),
            P(),
        ),
        out_specs=P(None, None, ("dom", "quad")),
        check_vma=False,
    )
```

time: 70 us -> 52.6 us (0.75)
  Pallas kernels: 63.9 us -> 50.6 us
  local copies, waits for them, and re-layouts: 2.5 us -> 0.01 us
  other arithmetic: 3.15 us -> 1.89 us
    pallas_call x3 -> x1, Pallas kernels: 63.9 us -> 50.6 us  [step(): pl.pallas_call(step_body, out_shape=jax.ShapeDtypeStruct((QUANT, BASIS, E...]
    concatenate x3 -> x0, other arithmetic: 2.17 us -> none  [parts(): return jnp.concatenate([high, high, weights - high], axis=-1).astype(bf16)]
    add x0 -> x1, other arithmetic: none -> 1.89 us  [local(): return element_dofs + jnp.transpose(change, (1, 0, 2))]
    reshape x4 -> x0, local copies, waits for them, and re-layouts: 1.49 us -> none  [the longest x1 0.79 us: weights_of(): face_projection.reshape(4, 3, 7, BASIS)]
    unnamed x7 -> x2, local copies, waits for them, and re-layouts: 0.99 us -> 0.01 us
    another operation x3 -> x0, other arithmetic: 0.98 us -> none
where the time goes in v1:
time: 52.6 us; the launch traced here: 52.5 us
  Pallas kernels  50.6 us (96%)
  other arithmetic  1.89 us (4%)
    pallas_call x1, Pallas kernels, step(): pl.pallas_call(step_body, out_shape=jax.ShapeDtypeStruct((QUANT, BASIS, E...  50.6 us
    add x1, other arithmetic, local(): return element_dofs + jnp.transpose(change, (1, 0, 2))  1.89 us

profile of v1, /device:TPU:1, one launch (start us, length us, event | category | flops | bytes accessed | tf_op | source)
XLA Modules:
  0.0 52.5 jit_solution(3904775022829952182)
XLA Ops:
  0.0 0.0 copy-start
  0.0 50.6 %shard_map.136 = f32[9,56,256]{2,1,0:T(8,128)} custom-call(f32[9,56,256]{2,1,0:T(8,128)} %bitcast.13, f32[9,9,3,256]{3,2,1,0:T(4,128)} %bitcast.14, f32[168,56]{1,0:T(8,128)} %bitcast.15, f32[21,4,56]{2,1,0:T(4,128)} %bitcast.17, f32[21,4,56]{2,1,0:T(4,128)} %bitcast.18, f32[3,4,256]{2,1,0:T(4,128)} %normals_ref.1, f32[1,256]{1,0:T(1,128)} %bitcast.19, ...), custom_call_target="tpu_custom_call" | custom-call | tf_op jit(solution)/shard_map/pallas_call | solution.py:495
  50.6 0.0 copy-done
  50.6 1.9 %bitcast_add_fusion = f32[56,9,256]{2,0,1:T(8,128)} fusion(f32[56,9,256]{2,0,1:T(8,128)S(1)} %copy-done, f32[9,56,256]{2,1,0:T(8,128)} %shard_map.136), kind=kLoop, calls=%fused_computation | loop fusion | flops 129024 | bytes 1548288 | tf_op jit(solution)/shard_map/add | solution.py:543
Async XLA Ops:
  0.0 50.6 %copy-start = (f32[56,9,256]{2,0,1:T(8,128)S(1)}, f32[56,9,256]{2,0,1:T(8,128)}, u32[]{:S(2)}) copy-start(f32[56,9,256]{2,0,1:T(8,128)} %param.14) | copy-start | bytes 1548292

commit v2 on v1

--- a/solution.py
+++ b/solution.py
@@ -19,9 +19,11 @@
 WIRE = 192
 CODE, PARTNER = 189, 190
 PIECES = 4
+DIRECT = (3,)
+OFFSETS = [(dz, dx) for dz in (0, 1, 7, 2, 6, 3, 5, 4) for dx in (0, 1, 3, 2)]
 f32, bf16 = jnp.float32, jnp.bfloat16
 MESH = pl.DeviceIdType.MESH
-VMEM_LIMIT = 56 * 1024 * 1024
+VMEM_LIMIT = 32 * 1024 * 1024
 
 
 def iota(shape, dim):
@@ -193,7 +195,7 @@
 def step_body(
     x_ref, star_in, stiff_ref, proj_in, lift_in, normals_ref, speed_ref, index_ref, orient_ref, send_ref, face_ref,
     dest_ref, region_ref, table_ref,
-    change_ref,
+    updated_ref,
     star, kmat, proj, lift, mixed, deriv, integral, volume, trace, table, slots, raw, matrix, fluxes, points, params,
     rows, held, replies, back, halo_out, halo_in,
     halo_send, halo_recv, out_send, out_recv, ring_send, ring_recv, side_send, side_recv, back_send, back_recv, local_sem,
@@ -207,23 +209,23 @@
     def slot(yy, cc):
         return yy * 2 + cc
 
-    def peer(o):
-        return ((o // 4) * 8 + member, o % 4)
+    def peer(i, sign):
+        dz, dx = OFFSETS[i]
+        zz, xx = lax.rem(block + (8 + sign * dz) % 8, 8), lax.rem(quad + (4 + sign * dx) % 4, 4)
+        return zz * 4 + xx, (zz * 8 + member, xx)
 
     up, down, far = (y + 1) % 4, (y + 3) % 4, (y + 2) % 4
     mem_up, mem_down, mem_far = slot(up, core), slot(down, core), slot(far, core)
     to_up, to_down = (block * 8 + mem_up, quad), (block * 8 + mem_down, quad)
+    to_far = (block * 8 + mem_far, quad)
     to_side = (block * 8 + slot(y, 1 - core), quad)
     upper, lower = (lax.rem(dom + 1, doms), quad), (lax.rem(dom + doms - 1, doms), quad)
 
     barrier = pltpu.get_barrier_semaphore()
 
-    def greet(i, carry):
-        pl.semaphore_signal(barrier, inc=1, device_id=peer(lax.rem(own + i, 32)), device_id_type=MESH)
-        return carry
-
-    lax.fori_loop(1, 32, greet, 0)
-    for device in (to_up, to_down, to_side, upper, lower):
+    for i in range(31, 0, -1):
+        pl.semaphore_signal(barrier, inc=1, device_id=peer(i, -1)[1], device_id_type=MESH)
+    for device in (to_up, to_down, to_side, to_far, upper, lower):
         pl.semaphore_signal(barrier, inc=1, device_id=device, device_id_type=MESH)
 
     for q in range(QUANT):
@@ -252,7 +254,7 @@
         integral[r] = value
 
     def degree(k, scale):
-        scale = scale / (k + 1).astype(f32)
+        scale = scale / (k + 1)
 
         def store(q, lanes, value):
             deriv[q, :, lanes] = value
@@ -263,7 +265,9 @@
             spatial_mix(tile, (0, 3, 6), star, mixed, store)
         return scale
 
-    lax.fori_loop(1, ORDER, degree, jnp.float32(1.0))
+    scale = 1.0
+    for k in range(1, ORDER):
+        scale = degree(k, scale)
 
     for r in range(QUANT):
         traced = dot(proj[...], split3(integral[r]))
@@ -285,16 +289,12 @@
             src_ref=src, dst_ref=dst, send_sem=send_sem, recv_sem=recv_sem, device_id=device, device_id_type=MESH
         )
 
-    pl.semaphore_wait(barrier, 31 + 5)
+    pl.semaphore_wait(barrier, 31 + 6)
     per = 32 // PIECES
 
-    for piece in range(PIECES):
-        def push(i, carry, piece=piece):
-            o = lax.rem(own + i, 32)
-            remote(rows.at[o], held.at[member, i], out_send, out_recv.at[piece], peer(o)).start()
-            return carry
-
-        lax.fori_loop(max(1, piece * per), (piece + 1) * per, push, 0)
+    for i in range(31, 0, -1):
+        o, device = peer(i, 1)
+        remote(rows.at[o], held.at[member, i], out_send, out_recv.at[i // per], device).start()
     mine = pltpu.make_async_copy(rows.at[own], held.at[member, 0], local_sem)
     mine.start()
 
@@ -322,14 +322,16 @@
         go(ring(member, piece, piece, to_up))
         go(ring(member, piece, PIECES + piece, to_down))
         go(side(member, piece, piece))
+        if piece in DIRECT:
+            go(ring(member, piece, 2 * PIECES + piece, to_far))
 
     def ring_piece(piece):
         ring(mem_down, piece, piece, to_up).wait_recv()
-        if piece % 2 == 0:
+        if piece % 2 == 0 and piece not in DIRECT:
             go(ring(mem_down, piece, 2 * PIECES + piece, to_up))
         go(side(mem_down, piece, PIECES + piece))
         ring(mem_up, piece, PIECES + piece, to_down).wait_recv()
-        if piece % 2 == 1:
+        if piece % 2 == 1 and piece not in DIRECT:
             go(ring(mem_up, piece, 2 * PIECES + piece, to_down))
         go(side(mem_up, piece, 2 * PIECES + piece))
 
@@ -366,19 +368,10 @@
     high.start()
     for i, row in enumerate(friction_params(code_at, region_ref, table_ref)):
         params[pl.ds(i, 1), :] = row
-    own_piece(0)
-    own_neighbours(0)
-    own_piece(1)
-    own_neighbours(1)
-    own_piece(2)
-    ring_piece(0)
-    own_neighbours(2)
-    own_piece(3)
-    ring_piece(1)
-
-    want = unpacked(held, member)[1][:, PARTNER - 128 : PARTNER - 127]
-
-    def matched(m):
+    def wanted():
+        return unpacked(held, member)[1][:, PARTNER - 128 : PARTNER - 127]
+
+    def matched(m, want):
         first, second = unpacked(held, m)
         pick = one_hot(want == to_row(second[:, CODE - 128 : CODE - 127]))
         values = jnp.concatenate([first, second], axis=1)
@@ -386,33 +379,38 @@
         low_part = (values - high_part.astype(f32)).astype(bf16)
         return dot(pick, high_part) + dot(pick, low_part)
 
-    total = matched(member)
+    own_neighbours(0)
+    own_piece(0)
+    own_neighbours(1)
+    own_piece(1)
+    own_neighbours(2)
+    own_piece(2)
+    own_neighbours(3)
+    ring_piece(0)
+    own_piece(3)
+    ring_piece(1)
+    want = wanted()
+    total = matched(member, want)
     ring_piece(2)
-    own_neighbours(3)
+    far_piece(0)
     ring_piece(3)
-    far_piece(0)
-    total += matched(mem_down)
-    far_piece(1)
-    total += matched(mem_up)
-    far_piece(2)
+    total += matched(mem_down, want)
+    total += matched(mem_up, want)
     side_pieces(slot(y, 1 - core), 0)
-    total += matched(slot(y, 1 - core))
-    far_piece(3)
+    total += matched(slot(y, 1 - core), want)
+    for piece in range(1, PIECES):
+        far_piece(piece)
     side_pieces(slot(down, 1 - core), 1)
-    total += matched(slot(down, 1 - core))
+    total += matched(slot(down, 1 - core), want)
     side_pieces(slot(up, 1 - core), 2)
-    total += matched(slot(up, 1 - core))
-    total += matched(mem_far)
+    total += matched(slot(up, 1 - core), want)
+    total += matched(mem_far, want)
     side_pieces(slot(far, 1 - core), 3)
-    total += matched(slot(far, 1 - core))
+    total += matched(slot(far, 1 - core), want)
     put_packed(replies, total[:, :128], total[:, 128:])
 
-    def reply(i, carry):
-        o = lax.rem(own + 32 - i, 32)
-        remote(replies.at[i], back.at[own], back_send, back_recv, peer(o)).start()
-        return carry
-
-    lax.fori_loop(1, 32, reply, 0)
+    for i in range(31, 0, -1):
+        remote(replies.at[i], back.at[own], back_send, back_recv, peer(i, -1)[1]).start()
     mine = pltpu.make_async_copy(replies.at[0], back.at[own], local_sem)
     mine.start()
 
@@ -487,7 +485,7 @@
                     fluxes[r, pl.ds(f * ROWS + 8 * chunk, 8), lanes] = flux
 
     for r in range(QUANT):
-        change_ref[r] = 0.25 * (volume[r] - dot(lift[...], split3(fluxes[r])))
+        updated_ref[r] = x_ref[r] + 0.25 * (volume[r] - dot(lift[...], split3(fluxes[r])))
 
 
 def step(*operands):
@@ -531,7 +529,7 @@
     element_dofs, star_matrices, face_normals, wave_speed, stiffness, face_projection, face_lift, friction_table,
     neighbour_index, orientation, send_list, fault_face, fault_dest, fault_region,
 ):
-    change = step(
+    updated = step(
         jnp.transpose(element_dofs, (1, 0, 2)),
         jnp.transpose(star_matrices, (1, 2, 0, 3)),
         jnp.transpose(stiffness, (1, 0, 2)).reshape(3 * BASIS, BASIS),
@@ -540,7 +538,7 @@
         face_normals, wave_speed.reshape(1, -1), neighbour_index, orientation, send_list,
         fault_face.reshape(1, -1), fault_dest.reshape(1, -1), fault_region.reshape(1, -1), friction_table,
     )
-    return element_dofs + jnp.transpose(change, (1, 0, 2))
+    return jnp.transpose(updated, (1, 0, 2))
 
 
 def solution(mesh):

time: 52.6 us -> 56.4 us (1.072)
  local copies, waits for them, and re-layouts: 0.01 us -> 10.2 us
  Pallas kernels: 50.6 us -> 45.6 us
  other arithmetic: 1.89 us -> 0 us
    unnamed x2 -> x29, local copies, waits for them, and re-layouts: 0.01 us -> 10.2 us
    pallas_call x1, Pallas kernels: 50.6 us -> 45.6 us  [step(): pl.pallas_call(step_body, out_shape=jax.ShapeDtypeStruct((QUANT, BASIS, E...]
    add x1 -> x0, other arithmetic: 1.89 us -> none  [local(): return element_dofs + jnp.transpose(change, (1, 0, 2))]
where the time goes in v2:
time: 56.4 us; the launch traced here: 55.9 us
  Pallas kernels  45.6 us (81%)
  local copies, waits for them, and re-layouts  10.2 us (18%)
    pallas_call x1, Pallas kernels, step(): pl.pallas_call(step_body, out_shape=jax.ShapeDtypeStruct((QUANT, BASIS, E...  45.6 us
    unnamed x29, local copies, waits for them, and re-layouts  10.2 us

profile of v2, /device:TPU:1, one launch (start us, length us, event | category | flops | bytes accessed | tf_op | source)
XLA Modules:
  0.0 55.9 jit_solution(3327804852653196345)
XLA Ops:
  0.0 0.0 copy-start.6
  0.0 0.0 copy-start.7
  0.0 0.0 copy-start.11
  0.0 0.7 %copy-done.6 = f32[3,4,256]{2,1,0:T(4,128)S(1)} copy-done((f32[3,4,256]{2,1,0:T(4,128)S(1)}, f32[3,4,256]{2,1,0:T(4,128)}, u32[]{:S(2)}) %copy-start.6) | copy-done | bytes 12312
  0.7 0.0 copy-done.7
  0.7 0.0 copy-done.11
  0.7 0.0 copy-start
  0.7 1.0 %copy-done = f32[56,9,256]{2,0,1:T(8,128)S(1)} copy-done((f32[56,9,256]{2,0,1:T(8,128)S(1)}, f32[56,9,256]{2,0,1:T(8,128)}, u32[]{:S(2)}) %copy-start) | copy-done | bytes 516120
  1.8 0.0 copy-start.1
  1.8 1.0 %copy-done.1 = f32[3,9,9,256]{3,0,2,1:T(4,128)S(1)} copy-done((f32[3,9,9,256]{3,0,2,1:T(4,128)S(1)}, f32[3,9,9,256]{3,0,2,1:T(4,128)}, u32[]{:S(2)}) %copy-start.1) | copy-done | bytes 248856
  2.7 0.0 copy-start.2
  2.7 0.9 %copy-done.2 = f32[56,3,56]{2,0,1:T(8,128)S(1)} copy-done((f32[56,3,56]{2,0,1:T(8,128)S(1)}, f32[56,3,56]{2,0,1:T(8,128)}, u32[]{:S(2)}) %copy-start.2) | copy-done | bytes 37656
  3.6 0.0 copy-start.3
  3.6 0.8 %copy-done.3 = s32[16384]{0:T(1024)S(1)} copy-done((s32[16384]{0:T(1024)S(1)}, s32[16384]{0:T(1024)}, u32[]{:S(2)}) %copy-start.3) | copy-done | bytes 65560
  4.5 0.0 copy-start.4
  4.5 0.8 %copy-done.4 = f32[4,21,56]{2,0,1:T(4,128)S(1)} copy-done((f32[4,21,56]{2,0,1:T(4,128)S(1)}, f32[4,21,56]{2,0,1:T(4,128)}, u32[]{:S(2)}) %copy-start.4) | copy-done | bytes 18840
  5.2 0.8 %copy-done.5 = f32[4,56,21]{1,0,2:T(4,128)S(1)} copy-done((f32[4,56,21]{1,0,2:T(4,128)S(1)}, f32[4,56,21]{1,0,2:T(4,128)}, u32[]{:S(2)}) %copy-start.5) | copy-done | bytes 18840
  6.0 0.7 %copy-done.8 = s32[4,256]{1,0:T(4,128)S(1)} copy-done((s32[4,256]{1,0:T(4,128)S(1)}, s32[4,256]{1,0:T(4,128)}, u32[]{:S(2)}) %copy-start.8) | copy-done | bytes 4120
  6.7 0.7 %copy-done.9 = s32[2,256]{1,0:T(2,128)S(1)} copy-done((s32[2,256]{1,0:T(2,128)S(1)}, s32[2,256]{1,0:T(2,128)}, u32[]{:S(2)}) %copy-start.9) | copy-done | bytes 2072
  7.4 0.7 %copy-done.10 = f32[3,8]{1,0:T(4,128)S(1)} copy-done((f32[3,8]{1,0:T(4,128)S(1)}, f32[3,8]{1,0:T(4,128)}, u32[]{:S(2)}) %copy-start.10) | copy-done | bytes 120
  8.1 0.7 %copy-done.12 = s32[256]{0:T(256)S(1)} copy-done((s32[256]{0:T(256)S(1)}, s32[256]{0:T(256)}, u32[]{:S(2)}) %copy-start.12) | copy-done | bytes 1048
  8.8 0.7 %copy-done.13 = s32[256]{0:T(256)S(1)} copy-done((s32[256]{0:T(256)S(1)}, s32[256]{0:T(256)}, u32[]{:S(2)}) %copy-start.13) | copy-done | bytes 1048
  9.4 45.6 %shard_map.136 = f32[9,56,256]{2,1,0:T(8,128)S(1)} custom-call(f32[9,56,256]{2,1,0:T(8,128)S(1)} %bitcast.13, f32[9,9,3,256]{3,2,1,0:T(4,128)S(1)} %bitcast.14, f32[168,56]{1,0:T(8,128)S(1)} %bitcast.15, f32[21,4,56]{2,1,0:T(4,128)S(1)} %bitcast.17, f32[21,4,56]{2,1,0:T(4,128)S(1)} %bitcast.18, f32[3,4,256]{2,1,0:T(4,128)S(1)} %copy-done.6, ...), custom_call_target="tpu_custom_call" | custom-call | tf_op jit(solution)/shard_map/pallas_call | solution.py:493
  55.1 0.8 %copy.16 = f32[56,9,256]{2,0,1:T(8,128)} copy(f32[56,9,256]{2,0,1:T(8,128)S(1)} %bitcast.12) | data formatting | bytes 1032192
  (6 shorter events, 0.0 us)
Async XLA Ops:
  0.0 0.7 %copy-start.6 = (f32[3,4,256]{2,1,0:T(4,128)S(1)}, f32[3,4,256]{2,1,0:T(4,128)}, u32[]{:S(2)}) copy-start(f32[3,4,256]{2,1,0:T(4,128)} %normals_ref.1) | copy-start | bytes 36868
  0.0 0.7 %copy-start.7 = (s32[4,256]{1,0:T(4,128)S(1)}, s32[4,256]{1,0:T(4,128)}, u32[]{:S(2)}) copy-start(s32[4,256]{1,0:T(4,128)} %index_ref.1) | copy-start | bytes 12292
  0.0 0.7 %copy-start.11 = (f32[256]{0:T(256)S(1)}, f32[256]{0:T(256)}, u32[]{:S(2)}) copy-start(f32[256]{0:T(256)} %param.17) | copy-start | bytes 3076
  0.7 1.0 %copy-start = (f32[56,9,256]{2,0,1:T(8,128)S(1)}, f32[56,9,256]{2,0,1:T(8,128)}, u32[]{:S(2)}) copy-start(f32[56,9,256]{2,0,1:T(8,128)} %param.14) | copy-start | bytes 1548292
  1.8 1.0 %copy-start.1 = (f32[3,9,9,256]{3,0,2,1:T(4,128)S(1)}, f32[3,9,9,256]{3,0,2,1:T(4,128)}, u32[]{:S(2)}) copy-start(f32[3,9,9,256]{3,0,2,1:T(4,128)} %param.15) | copy-start | bytes 746500
  2.7 0.9 %copy-start.2 = (f32[56,3,56]{2,0,1:T(8,128)S(1)}, f32[56,3,56]{2,0,1:T(8,128)}, u32[]{:S(2)}) copy-start(f32[56,3,56]{2,0,1:T(8,128)} %param.18) | copy-start | bytes 112900
  3.6 0.8 %copy-start.3 = (s32[16384]{0:T(1024)S(1)}, s32[16384]{0:T(1024)}, u32[]{:S(2)}) copy-start(s32[16384]{0:T(1024)} %param.27) | copy-start | bytes 196612
  4.5 0.8 %copy-start.4 = (f32[4,21,56]{2,0,1:T(4,128)S(1)}, f32[4,21,56]{2,0,1:T(4,128)}, u32[]{:S(2)}) copy-start(f32[4,21,56]{2,0,1:T(4,128)} %param.19) | copy-start | bytes 56452
  5.2 0.8 %copy-start.5 = (f32[4,56,21]{1,0,2:T(4,128)S(1)}, f32[4,56,21]{1,0,2:T(4,128)}, u32[]{:S(2)}) copy-start(f32[4,56,21]{1,0,2:T(4,128)} %param.20) | copy-start | bytes 56452
  6.0 0.7 %copy-start.8 = (s32[4,256]{1,0:T(4,128)S(1)}, s32[4,256]{1,0:T(4,128)}, u32[]{:S(2)}) copy-start(s32[4,256]{1,0:T(4,128)} %orient_ref.1) | copy-start | bytes 12292
  6.7 0.7 %copy-start.9 = (s32[2,256]{1,0:T(2,128)S(1)}, s32[2,256]{1,0:T(2,128)}, u32[]{:S(2)}) copy-start(s32[2,256]{1,0:T(2,128)} %send_ref.1) | copy-start | bytes 6148
  7.4 0.7 %copy-start.10 = (f32[3,8]{1,0:T(4,128)S(1)}, f32[3,8]{1,0:T(4,128)}, u32[]{:S(2)}) copy-start(f32[3,8]{1,0:T(4,128)} %table_ref.1) | copy-start | bytes 292
  8.1 0.7 %copy-start.12 = (s32[256]{0:T(256)S(1)}, s32[256]{0:T(256)}, u32[]{:S(2)}) copy-start(s32[256]{0:T(256)} %param.25) | copy-start | bytes 3076
  8.8 0.7 %copy-start.13 = (s32[256]{0:T(256)S(1)}, s32[256]{0:T(256)}, u32[]{:S(2)}) copy-start(s32[256]{0:T(256)} %param.26) | copy-start | bytes 3076

commit v3 on v2

--- a/solution.py
+++ b/solution.py
@@ -23,7 +23,7 @@
 OFFSETS = [(dz, dx) for dz in (0, 1, 7, 2, 6, 3, 5, 4) for dx in (0, 1, 3, 2)]
 f32, bf16 = jnp.float32, jnp.bfloat16
 MESH = pl.DeviceIdType.MESH
-VMEM_LIMIT = 32 * 1024 * 1024
+VMEM_LIMIT = 56 * 1024 * 1024
 
 
 def iota(shape, dim):
@@ -192,14 +192,19 @@
     return jnp.concatenate(parts, axis=1)
 
 
-def step_body(
-    x_ref, star_in, stiff_ref, proj_in, lift_in, normals_ref, speed_ref, index_ref, orient_ref, send_ref, face_ref,
-    dest_ref, region_ref, table_ref,
-    updated_ref,
-    star, kmat, proj, lift, mixed, deriv, integral, volume, trace, table, slots, raw, matrix, fluxes, points, params,
-    rows, held, replies, back, halo_out, halo_in,
-    halo_send, halo_recv, out_send, out_recv, ring_send, ring_recv, side_send, side_recv, back_send, back_recv, local_sem,
-):
+def step_body(*refs):
+    sources, refs = refs[:14], refs[14:]
+    copied, refs = refs[-14:], refs[:-14]
+    (
+        x_ref, star_in, stiff_ref, proj_in, lift_in, normals_ref, speed_ref, index_ref,
+        orient_ref, send_ref, face_ref, dest_ref, region_ref, table_ref,
+    ) = copied
+    (
+        updated_ref,
+        star, kmat, proj, lift, mixed, deriv, integral, volume, trace, table, slots, raw, matrix, fluxes, points, params,
+        rows, held, replies, back, halo_out, halo_in,
+        halo_send, halo_recv, out_send, out_recv, ring_send, ring_recv, side_send, side_recv, back_send, back_recv, local_sem, in_sem,
+    ) = refs
     dom, quad = lax.axis_index("dom"), lax.axis_index("quad")
     doms = lax.axis_size("dom")
     block, member = dom // 8, dom % 8
@@ -221,6 +226,10 @@
     to_side = (block * 8 + slot(y, 1 - core), quad)
     upper, lower = (lax.rem(dom + 1, doms), quad), (lax.rem(dom + doms - 1, doms), quad)
 
+    arriving = [pltpu.make_async_copy(source, held_in, in_sem.at[i]) for i, (source, held_in) in enumerate(zip(sources, copied))]
+    for copy in arriving:
+        copy.start()
+
     barrier = pltpu.get_barrier_semaphore()
 
     for i in range(31, 0, -1):
@@ -228,6 +237,8 @@
     for device in (to_up, to_down, to_side, to_far, upper, lower):
         pl.semaphore_signal(barrier, inc=1, device_id=device, device_id_type=MESH)
 
+    for copy in arriving:
+        copy.wait()
     for q in range(QUANT):
         for r in range(QUANT):
             star[:, q, r, :] = star_in[q, r]
@@ -492,8 +503,8 @@
     vmem, dma = pl.BlockSpec(memory_space=pltpu.VMEM), pltpu.SemaphoreType.DMA
     return pl.pallas_call(
         step_body,
-        out_shape=jax.ShapeDtypeStruct((QUANT, BASIS, ELEM), f32),
-        in_specs=[vmem] * 13 + [pl.BlockSpec(memory_space=pltpu.SMEM)],
+        out_shape=pltpu.VMEM((QUANT, BASIS, ELEM), f32),
+        in_specs=[pl.BlockSpec(memory_space=pltpu.HBM)] * 14,
         out_specs=vmem,
         scratch_shapes=[
             pltpu.VMEM((3, QUANT, QUANT, ELEM), f32),
@@ -519,7 +530,9 @@
             pltpu.VMEM((2, COMPS, 256), f32),
             pltpu.VMEM((2, COMPS, 256), f32),
             dma((2,)), dma((2,)), dma, dma((PIECES,)), dma((3 * PIECES,)), dma((3 * PIECES,)),
-            dma((4 * PIECES,)), dma((4 * PIECES,)), dma, dma, dma,
+            dma((4 * PIECES,)), dma((4 * PIECES,)), dma, dma, dma, dma((14,)),
+            *[pltpu.VMEM(o.shape, o.dtype) for o in operands[:13]],
+            pltpu.SMEM(operands[13].shape, f32),
         ],
         compiler_params=pltpu.CompilerParams(collective_id=0, has_side_effects=True, vmem_limit_bytes=VMEM_LIMIT),
     )(*operands)

time: 56.4 us -> 47.1 us (0.84)
  local copies, waits for them, and re-layouts: 10.2 us -> 0.79 us
  Pallas kernels: 45.6 us -> 46.2 us
    unnamed x29 -> x1, local copies, waits for them, and re-layouts: 10.2 us -> 0.79 us
where the time goes in v3:
time: 47.1 us; the launch traced here: 47 us
  Pallas kernels  46.2 us (98%)
  local copies, waits for them, and re-layouts  0.79 us (2%)
    pallas_call x1, Pallas kernels, step(): pl.pallas_call(step_body, out_shape=pltpu.VMEM((QUANT, BASIS, ELEM), f32)...  46.2 us

profile of v3, /device:TPU:1, one launch (start us, length us, event | category | flops | bytes accessed | tf_op | source)
XLA Modules:
  0.0 47.0 jit_solution(8820054526437673865)
XLA Ops:
  0.0 46.2 %shard_map.136 = f32[9,56,256]{2,1,0:T(8,128)S(1)} custom-call(f32[9,56,256]{2,1,0:T(8,128)} %bitcast.13, f32[9,9,3,256]{3,2,1,0:T(4,128)} %bitcast.14, f32[168,56]{1,0:T(8,128)} %bitcast.15, f32[21,4,56]{2,1,0:T(4,128)} %bitcast.17, f32[21,4,56]{2,1,0:T(4,128)} %bitcast.18, f32[3,4,256]{2,1,0:T(4,128)} %refs_5_.1, f32[1,256]{1,0:T(1,128)} %bitcast.19, ...), custom_call_target="tpu_custom_call" | custom-call | tf_op jit(solution)/shard_map/pallas_call | solution.py:504
  46.2 0.8 %copy.16 = f32[56,9,256]{2,0,1:T(8,128)} copy(f32[56,9,256]{2,0,1:T(8,128)S(1)} %bitcast.12) | data formatting | bytes 1032192

commit v4 on v3

--- a/solution.py
+++ b/solution.py
@@ -134,12 +134,6 @@
             store(first + i, lanes, total[i])
 
 
-def inverse_sinh(value):
-    magnitude = jnp.abs(value)
-    result = jnp.log(magnitude + jnp.sqrt(1.0 + magnitude * magnitude))
-    return jnp.where(value < 0.0, -result, result)
-
-
 def friction_params(code_at, region_ref, table_ref):
     code_col = to_col(code_at).astype(jnp.int32)
     pairs = region_ref.shape[1] // 32
@@ -174,8 +168,10 @@
     slip = jnp.zeros_like(locked)
     for _ in range(NEWTON):
         argument = stiff_rate * slip
-        mismatch = 0.5 * slip + pressure * rate_term * inverse_sinh(argument) - locked
-        gradient = 0.5 + pressure * rate_term * stiff_rate / jnp.sqrt(1.0 + argument * argument)
+        root = jnp.sqrt(1.0 + argument * argument)
+        arsinh = jnp.log(jnp.abs(argument) + root)
+        mismatch = 0.5 * slip + pressure * rate_term * jnp.where(argument < 0.0, -arsinh, arsinh) - locked
+        gradient = 0.5 + pressure * rate_term * stiff_rate / root
         slip = slip - 0.4 * mismatch / gradient
     third = 2.0 * (locked - 0.5 * slip - background) - comp(own, 3)
     seventh = comp(other, 7) - sign * slip
@@ -202,7 +198,7 @@
     (
         updated_ref,
         star, kmat, proj, lift, mixed, deriv, integral, volume, trace, table, slots, raw, matrix, fluxes, points, params,
-        rows, held, replies, back, halo_out, halo_in,
+        rows, held, replies, back, halo_out, halo_in, placed,
         halo_send, halo_recv, out_send, out_recv, ring_send, ring_recv, side_send, side_recv, back_send, back_recv, local_sem, in_sem,
     ) = refs
     dom, quad = lax.axis_index("dom"), lax.axis_index("quad")
@@ -248,15 +244,21 @@
         for p in range(21):
             padded[:, p // 7 * 8 + p % 7, :] = source[p]
     proj[...] = weight_parts(points[0].reshape(4 * ROWS, BASIS))
-    lift[...] = weight_parts(
-        jnp.concatenate(
-            [
-                jnp.concatenate([points[1].reshape(4 * ROWS, BASIS), jnp.zeros((4 * ROWS, 128 - BASIS), f32)], axis=1),
-                jnp.zeros((128 - 4 * ROWS, 128), f32),
-            ],
-            axis=0,
-        ).T[:BASIS, : 4 * ROWS]
-    )
+    turned = jnp.concatenate(
+        [
+            jnp.concatenate([points[1].reshape(4 * ROWS, BASIS), jnp.zeros((4 * ROWS, 128 - BASIS), f32)], axis=1),
+            jnp.zeros((128 - 4 * ROWS, 128), f32),
+        ],
+        axis=0,
+    ).T[:BASIS, : 4 * ROWS]
+    turned_high = turned.astype(bf16).astype(f32)
+    lift[...] = jnp.concatenate(
+        [
+            jnp.concatenate([turned_high, turned_high], axis=1),
+            jnp.concatenate([turned - turned_high, jnp.zeros((BASIS, 4 * ROWS), f32)], axis=1),
+        ],
+        axis=0,
+    ).astype(bf16)
     face_at, code_at = slot_rows(dest_ref[...], face_ref[...])
 
     for r in range(QUANT):
@@ -406,15 +408,13 @@
     far_piece(0)
     ring_piece(3)
     total += matched(mem_down, want)
+    far_piece(1)
+    far_piece(3)
     total += matched(mem_up, want)
-    side_pieces(slot(y, 1 - core), 0)
-    total += matched(slot(y, 1 - core), want)
-    for piece in range(1, PIECES):
-        far_piece(piece)
-    side_pieces(slot(down, 1 - core), 1)
-    total += matched(slot(down, 1 - core), want)
-    side_pieces(slot(up, 1 - core), 2)
-    total += matched(slot(up, 1 - core), want)
+    far_piece(2)
+    for i, m in enumerate((slot(y, 1 - core), slot(down, 1 - core), slot(up, 1 - core))):
+        side_pieces(m, i)
+        total += matched(m, want)
     total += matched(mem_far, want)
     side_pieces(slot(far, 1 - core), 3)
     total += matched(slot(far, 1 - core), want)
@@ -463,12 +463,19 @@
     out_done = remote(rows.at[pl.ds(0, 31)], held.at[member, pl.ds(0, 31)], out_send, out_recv.at[0], to_up)
     out_done.wait_send()
     face_col = to_col(face_at).astype(jnp.int32)
+    for f in range(4):
+        cols = pl.ds(f * ELEM, ELEM)
+        put = face_col == iota((256, ELEM), 1) + f * ELEM
+        placed[:, cols] = one_hot(put)
+        is_fault = jnp.sum(jnp.where(put, 1.0, 0.0), axis=0, keepdims=True) > 0.5
+        outer[:, cols] = jnp.where(is_fault, 0.0, outer[:, cols])
+    widening = widen()
     mine.wait()
     returned = remote(replies.at[pl.ds(0, 31)], back.at[pl.ds(0, 31)], back_send, back_recv, to_up)
     returned.wait_send()
     returned.wait_recv()
     first, second = unpacked(back)
-    other = dot(widen(), split2(jnp.concatenate([first.T, second.T[: WIRE - 128]], axis=0)))
+    other = dot(widening, split2(jnp.concatenate([first.T, second.T[: WIRE - 128]], axis=0)))
     law = [params[pl.ds(i, 1), :] for i in range(3)]
     imposed = split2(
         jnp.concatenate(
@@ -478,10 +485,7 @@
 
     for f in range(4):
         cols = pl.ds(f * ELEM, ELEM)
-        put = face_col == iota((256, ELEM), 1) + f * ELEM
-        fault = halves(dot(imposed, one_hot(put)))
-        is_fault = jnp.sum(jnp.where(put, 1.0, 0.0), axis=0, keepdims=True) > 0.5
-        outer[:, cols] = jnp.where(is_fault, fault, outer[:, cols])
+        outer[:, cols] += halves(dot(imposed, placed[:, cols]))
         for tile in range(ELEM // 128):
             lanes = pl.ds(tile * 128, 128)
             cols = pl.ds(f * ELEM + tile * 128, 128)
@@ -496,7 +500,7 @@
                     fluxes[r, pl.ds(f * ROWS + 8 * chunk, 8), lanes] = flux
 
     for r in range(QUANT):
-        updated_ref[r] = x_ref[r] + 0.25 * (volume[r] - dot(lift[...], split3(fluxes[r])))
+        updated_ref[r] = x_ref[r] + 0.25 * (volume[r] - halves(dot(lift[...], split2(fluxes[r]))))
 
 
 def step(*operands):
@@ -510,7 +514,7 @@
             pltpu.VMEM((3, QUANT, QUANT, ELEM), f32),
             pltpu.VMEM((3 * BASIS, 3 * BASIS), bf16),
             pltpu.VMEM((4 * ROWS, 3 * BASIS), bf16),
-            pltpu.VMEM((BASIS, 12 * ROWS), bf16),
+            pltpu.VMEM((2 * BASIS, 8 * ROWS), bf16),
             pltpu.VMEM((QUANT, 3 * BASIS, ELEM), f32),
             pltpu.VMEM((QUANT, BASIS, ELEM), f32),
             pltpu.VMEM((QUANT, BASIS, ELEM), f32),
@@ -529,6 +533,7 @@
             pltpu.VMEM((32, 12, 128), f32),
             pltpu.VMEM((2, COMPS, 256), f32),
             pltpu.VMEM((2, COMPS, 256), f32),
+            pltpu.VMEM((256, COLS), bf16),
             dma((2,)), dma((2,)), dma, dma((PIECES,)), dma((3 * PIECES,)), dma((3 * PIECES,)),
             dma((4 * PIECES,)), dma((4 * PIECES,)), dma, dma, dma, dma((14,)),
             *[pltpu.VMEM(o.shape, o.dtype) for o in operands[:13]],

time: 47.1 us -> 46.7 us (level)
  no operation moved by 1% of the time
where the time goes in v4:
time: 46.7 us; the launch traced here: 46.6 us
  Pallas kernels  45.8 us (98%)
  local copies, waits for them, and re-layouts  0.79 us (2%)
    pallas_call x1, Pallas kernels, step(): pl.pallas_call(step_body, out_shape=pltpu.VMEM((QUANT, BASIS, ELEM), f32)...  45.8 us

profile of v4, /device:TPU:1, one launch (start us, length us, event | category | flops | bytes accessed | tf_op | source)
XLA Modules:
  0.0 46.6 jit_solution(1890992463053586792)
XLA Ops:
  0.0 45.8 %shard_map.136 = f32[9,56,256]{2,1,0:T(8,128)S(1)} custom-call(f32[9,56,256]{2,1,0:T(8,128)} %bitcast.13, f32[9,9,3,256]{3,2,1,0:T(4,128)} %bitcast.14, f32[168,56]{1,0:T(8,128)} %bitcast.15, f32[21,4,56]{2,1,0:T(4,128)} %bitcast.17, f32[21,4,56]{2,1,0:T(4,128)} %bitcast.18, f32[3,4,256]{2,1,0:T(4,128)} %refs_5_.1, f32[1,256]{1,0:T(1,128)} %bitcast.19, ...), custom_call_target="tpu_custom_call" | custom-call | tf_op jit(solution)/shard_map/pallas_call | solution.py:508
  45.8 0.8 %copy.16 = f32[56,9,256]{2,0,1:T(8,128)} copy(f32[56,9,256]{2,0,1:T(8,128)S(1)} %bitcast.12) | data formatting | bytes 1032192
